TPU v7x, 32 devices: a whole 2x2x4 slice. The times are simulated.
32 devices in a mesh: leaf: 8 (over z, y), front: 4 (over x, core).
Axes of the slice: x: 2, y: 2, z: 4, core: 2. Of those that a mesh axis runs over, the one named last changes fastest.
Arguments:
- rhs_sub: float32 [8, 65536], P(None, ('leaf', 'front')), may hold values from -6 to 6
- rhs_sep: float32 [8, 16384], P(None, 'leaf'), may hold values from -6 to 6
- live_rows: int32 [32], P(('leaf', 'front')), may hold values from 256 to 2048, as said below
- lower_inv: bfloat16 [256, 256, 256], P(('leaf', 'front')), as said below
- upper_inv: bfloat16 [256, 256, 256], P(('leaf', 'front'))
- couple_low: bfloat16 [2048, 16384], P(('leaf', 'front')), may hold values from -0.25 to 0.25
- couple_up: bfloat16 [2048, 16384], P(('leaf', 'front')), may hold values from -0.046875 to 0.046875
- sep_lower_inv: bfloat16 [16384, 16384], P('leaf', 'front')
- sep_upper_inv: bfloat16 [16384, 16384], P('leaf', 'front')
- basis_sub: float32 [48, 65536], P(None, ('leaf', 'front')), may hold values from -0.01953125 to 0.01953125
- basis_sep: float32 [48, 16384], P(None, 'leaf'), may hold values from -0.01953125 to 0.01953125
Outputs:
- orth_sub: float32 [8, 65536], P(None, ('leaf', 'front'))
- orth_sep: float32 [8, 16384], P(None, 'leaf')
- coef: float32 [48, 8], replicated
Inputs may be any that keep to these rules, and one draw needn't show every extreme that they name: `live_rows`: each entry is a multiple of 256; some device has all 2048 rows live. Every block of lower_inv is lower triangular, and every block of upper_inv, sep_lower_inv and sep_upper_inv upper triangular, each with a diagonal between 1 and 1.5.
All inputs are finite; a program needn't handle non-finite values.
Results may differ from a plain program's by a relative error of at most 0.0055.
Values may be sent and summed in bfloat16 or wider, within the bound.
A program may use at most 128 MiB of HBM per device.

v0:
```python
import jax
import jax.numpy as jnp
from jax import lax
from jax.sharding import PartitionSpec as P


def apply_blocks(vectors, inverse):
    vec_count = vectors.shape[0]
    shaped = vectors.astype(jnp.bfloat16).reshape(vec_count, inverse.shape[0], inverse.shape[1])
    product = jnp.einsum("vkr,krc->vkc", shaped, inverse, preferred_element_type=jnp.float32)
    return product.reshape(vec_count, inverse.shape[0] * inverse.shape[2])


def shards(
    rhs_sub,
    rhs_sep,
    live_rows,
    lower_inv,
    upper_inv,
    couple_low,
    couple_up,
    sep_lower_inv,
    sep_upper_inv,
    basis_sub,
    basis_sep,
):
    vec_count, row_count = rhs_sub.shape
    border = couple_low.shape[0]
    high = lax.Precision.HIGHEST
    live_mask = lax.broadcasted_iota(jnp.int32, (1, row_count), 1) < live_rows[0]
    lower_sol = jnp.where(live_mask, apply_blocks(rhs_sub, lower_inv), 0.0)
    border_rows = lower_sol[:, :border].astype(jnp.bfloat16)
    columns = couple_low
    top_block = lax.psum_scatter(
        lax.dot_general(
            columns, border_rows, (((0,), (1,)), ((), ())), preferred_element_type=jnp.float32
        ),
        "leaf",
        scatter_dimension=0,
        tiled=True,
    )
    top_block = lax.psum(top_block, "front")
    top_rhs = rhs_sep - top_block.T
    lower_part = jnp.dot(
        top_rhs.astype(jnp.bfloat16), sep_lower_inv, preferred_element_type=jnp.float32
    )
    top_lower = lax.psum(lower_part, "leaf")
    upper_part = lax.dot_general(
        top_lower.astype(jnp.bfloat16),
        sep_upper_inv,
        (((1,), (1,)), ((), ())),
        preferred_element_type=jnp.float32,
    )
    top_sol = lax.psum(upper_part, "front")
    columns = couple_up
    correction = lax.dot_general(
        lax.all_gather(top_sol.astype(jnp.bfloat16), "leaf", axis=1, tiled=True),
        columns,
        (((1,), (1,)), ((), ())),
        preferred_element_type=jnp.float32,
    )
    updated = jnp.concatenate([lower_sol[:, :border] - correction, lower_sol[:, border:]], axis=1)
    upper_sol = jnp.where(live_mask, apply_blocks(updated, upper_inv), 0.0)
    coef_sum = jnp.zeros((basis_sub.shape[0], vec_count), jnp.float32)
    for sweep in range(2):
        local_sub = lax.dot_general(basis_sub, upper_sol, (((1,), (1,)), ((), ())), precision=high)
        local_sep = lax.dot_general(basis_sep, top_sol, (((1,), (1,)), ((), ())), precision=high)
        coef_pass = lax.psum(local_sub, ("leaf", "front")) + lax.psum(local_sep, "leaf")
        part_sub = upper_sol
        part_sep = top_sol
        part_sub = part_sub - lax.dot_general(
            coef_pass, basis_sub, (((0,), (0,)), ((), ())), precision=high
        )
        part_sep = part_sep - lax.dot_general(
            coef_pass, basis_sep, (((0,), (0,)), ((), ())), precision=high
        )
        upper_sol = part_sub
        top_sol = part_sep
        coef_sum = coef_sum + coef_pass
    return (upper_sol, top_sol, coef_sum)


def solution(mesh):
    return jax.shard_map(
        shards,
        mesh=mesh,
        in_specs=(
            P(None, ("leaf", "front")),
            P(None, "leaf"),
            P(("leaf", "front")),
            P(("leaf", "front"), None, None),
            P(("leaf", "front"), None, None),
            P(("leaf", "front"), None),
            P(("leaf", "front"), None),
            P("leaf", "front"),
            P("leaf", "front"),
            P(None, ("leaf", "front")),
            P(None, "leaf"),
        ),
        out_specs=(P(None, ("leaf", "front")), P(None, "leaf"), P()),
        check_vma=False,
    )
```

profile of v0, /device:TPU:0, one launch (start us, length us, event | category | flops | bytes accessed | tf_op | source)
XLA Modules:
  0.0 359.5 jit_solution(7207521694659329734)
XLA Ops:
  7.2 0.0 copy-start
  7.2 0.0 reduce-scatter.2.cloned.1.call-start
  8.0 0.8 convert_element_type.20
  8.9 1.5 fusion.10
  10.4 0.0 copy-done
  10.4 1.2 convolution_bitcast_fusion
  11.5 0.0 reduce-scatter.2.cloned.1.call-update
  11.6 0.0 all-reduce.4.cloned.1.call-start
  11.6 65.2 %reduce-scatter.2.cloned.1.call-done = f32[2048,8]{0,1:T(8,128)} async-done(((f32[16384,8]{0,1:T(8,128)}), f32[2048,8]{0,1:T(8,128)}) %reduce-scatter.2.cloned.1.call-update) | async-done | bytes 65552 | tf_op jit(solution)/shard_map/reduce_scatter | solution.py:34
  76.8 0.0 all-reduce.4.cloned.1.call-update
  76.8 0.0 copy-start.2
  76.8 0.0 copy-start.1
  76.8 0.0 all-reduce.6.cloned.1.call-start
  76.9 32.4 %all-reduce.4.cloned.1.call-done = f32[8,2048]{1,0:T(8,128)} async-done(((f32[8,2048]{1,0:T(8,128)}), f32[8,2048]{1,0:T(8,128)}) %all-reduce.4.cloned.1.call-update) | async-done | bytes 65552 | tf_op jit(solution)/shard_map/psum | solution.py:42
  109.3 8.1 %fusion.4 = f32[8,4096]{1,0:T(8,128)S(1)} fusion(bf16[2048,4096]{1,0:T(8,128)(2,1)} %param.18, f32[8,2048]{1,0:T(8,128)} %param.12, f32[8,2048]{1,0:T(8,128)} %all-reduce.4.cloned.1.call-done), kind=kOutput, calls=%fused_computation.16 | convolution fusion | flops 134250496 | bytes 17039360 | tf_op jit(solution)/shard_map/dot_general | solution.py:44
  117.4 38.4 %all-reduce.7 = bf16[8,4096]{1,0:T(8,128)(2,1)S(1)} all-reduce(f32[8,4096]{1,0:T(8,128)S(1)} %fusion.4), channel_id=1, replica_groups=mesh['leaf'=8,'front'=4] {'leaf'}, use_global_device_ids=true, to_apply=%region_2.3 | all-reduce | flops 32768 | bytes 196608 | tf_op jit(solution)/shard_map/psum | solution.py:47
  155.8 10.8 %fusion.12 = f32[8,2048]{1,0:T(8,128)} fusion(bf16[8,4096]{1,0:T(8,128)(2,1)S(1)} %all-reduce.7, bf16[2048,4096]{1,0:T(8,128)(2,1)} %param.19), kind=kOutput, calls=%fused_computation.29 | convolution fusion | flops 134217728 | bytes 16908288 | tf_op jit(solution)/shard_map/dot_general | solution.py:48
  166.7 0.0 all-reduce.6.cloned.1.call-update
  166.7 0.1 slice.16
  166.8 27.5 %all-reduce.6.cloned.1.call-done = f32[8,2048]{1,0:T(8,128)} async-done(((f32[8,2048]{1,0:T(8,128)}), f32[8,2048]{1,0:T(8,128)}) %all-reduce.6.cloned.1.call-update) | async-done | bytes 65552 | tf_op jit(solution)/shard_map/psum | solution.py:54
  194.2 0.8 convert_element_type.24
  195.1 30.8 %all_gather.3 = bf16[8,16384]{1,0:T(8,128)(2,1)S(1)} all-gather(bf16[8,2048]{1,0:T(8,128)(2,1)S(1)} %convert_element_type.24), channel_id=1, replica_groups=mesh['leaf'=8,'front'=4] {'leaf'}, dimensions={1}, use_global_device_ids=true | all-gather | bytes 294912 | tf_op jit(solution)/shard_map/all_gather | solution.py:57
  225.9 2.2 fusion
  228.1 0.1 pad_maximum_fusion
  228.2 1.5 fusion.11
  229.7 0.0 copy-done.2
  229.7 0.4 convolution_bitcast_fusion.4
  230.1 38.5 %psum.52 = f32[48,8]{0,1:T(8,128)S(1)} all-reduce(f32[48,8]{0,1:T(8,128)S(1)} %convolution_bitcast_fusion.4), channel_id=1, replica_groups=mesh['leaf'=8,'front'=4] {'leaf','front'}, use_global_device_ids=true, to_apply=%region_4.5 | all-reduce | flops 384 | bytes 3072 | tf_op jit(solution)/shard_map/psum | solution.py:68
  268.6 0.0 copy-done.1
  268.6 1.2 convolution_bitcast_fusion.3
  269.9 20.4 %psum.53 = f32[48,8]{0,1:T(8,128)S(1)} all-reduce(f32[48,8]{0,1:T(8,128)S(1)} %convolution_bitcast_fusion.3), channel_id=1, replica_groups=mesh['leaf'=8,'front'=4] {'leaf'}, use_global_device_ids=true, to_apply=%region_5.6 | all-reduce | flops 384 | bytes 3072 | tf_op jit(solution)/shard_map/psum | solution.py:68
  290.2 0.3 convolution_subtract_fusion.3
  290.6 0.4 convolution_bitcast_fusion.2
  291.0 36.9 %psum.54 = f32[48,8]{0,1:T(8,128)S(1)} all-reduce(f32[48,8]{0,1:T(8,128)S(1)} %convolution_bitcast_fusion.2), channel_id=1, replica_groups=mesh['leaf'=8,'front'=4] {'leaf','front'}, use_global_device_ids=true, to_apply=%region_6.7 | all-reduce | flops 384 | bytes 3072 | tf_op jit(solution)/shard_map/psum | solution.py:68
  327.8 1.1 convolution_subtract_fusion.2
  329.0 0.4 convolution_bitcast_fusion.1
  329.4 21.1 %psum.55 = f32[48,8]{0,1:T(8,128)S(1)} all-reduce(f32[48,8]{0,1:T(8,128)S(1)} %convolution_bitcast_fusion.1), channel_id=1, replica_groups=mesh['leaf'=8,'front'=4] {'leaf'}, use_global_device_ids=true, to_apply=%region_7.8 | all-reduce | flops 384 | bytes 3072 | tf_op jit(solution)/shard_map/psum | solution.py:68
  350.5 0.6 add_add_fusion
  351.1 0.9 convolution_subtract_fusion
  352.0 0.9 convolution_subtract_fusion.1
  (3 shorter events, 0.0 us)
Async XLA Ops:
  7.2 3.2 copy-start
  7.2 69.6 %reduce-scatter.2.cloned.1.call-start = ((), (), s32[]{:S(2)}) async-start(), calls=%async_computation.1 | async-start | bytes 589824 | tf_op jit(solution)/shard_map/reduce_scatter | solution.py:34
  11.6 97.7 %all-reduce.4.cloned.1.call-start = ((), (), s32[]{:S(2)}) async-start(), calls=%async_computation.2 | async-start | bytes 131072 | tf_op jit(solution)/shard_map/psum | solution.py:42
  76.8 152.9 %copy-start.2 = (f32[48,2048]{1,0:T(8,128)S(1)}, f32[48,2048]{1,0:T(8,128)}, u32[]{:S(2)}) copy-start(f32[48,2048]{1,0:T(8,128)} %param.20) | copy-start | bytes 1179652
  76.8 191.8 %copy-start.1 = (f32[48,2048]{1,0:T(8,128)S(1)}, f32[48,2048]{1,0:T(8,128)}, u32[]{:S(2)}) copy-start(f32[48,2048]{1,0:T(8,128)} %param.21) | copy-start | bytes 1179652
  76.8 117.4 %all-reduce.6.cloned.1.call-start = ((), (), s32[]{:S(2)}) async-start(), calls=%async_computation.3 | async-start | bytes 131072 | tf_op jit(solution)/shard_map/psum | solution.py:54
Sparse Core Ops, SparseCore 0:
  11.7 65.0 reduce-scatter.1
  79.2 30.0 all-reduce.3
  166.8 27.3 all-reduce.5
where the time goes:
time: 360 us
  blocking collectives  186 us (52%)
  waiting for transfers between devices  125 us (35%)
  matrix products  31.1 us (9%)
  between operations  14.6 us (4%)
    psum x2, blocking collectives, shards(): lax.psum(local_sub, ('leaf', 'front')) + lax.psum(local_sep, 'leaf')  75.4 us
    reduce_scatter x1, waiting for transfers between devices, shards(): lax.psum_scatter(lax.dot_general(columns, border_rows, (((0,), (1,)), (()...  65.2 us
    psum x2, blocking collectives, shards(): lax.psum(local_sep, 'leaf')  41.5 us
    psum x1, blocking collectives, shards(): top_lower = lax.psum(lower_part, 'leaf')  38.4 us
    psum x1, waiting for transfers between devices, shards(): top_block = lax.psum(top_block, 'front')  32.4 us
    all_gather x1, blocking collectives, shards(): lax.all_gather(top_sol.astype(jnp.bfloat16), 'leaf', axis=1, tiled=True)  30.8 us
    psum x1, waiting for transfers between devices, shards(): top_sol = lax.psum(upper_part, 'front')  27.5 us
    dot_general x1, matrix products, shards(): lax.dot_general(top_lower.astype(jnp.bfloat16), sep_upper_inv, (((1,), (1...  10.8 us
  transfers between devices with their start and end apart: 3, of which 3 were waited for; matrix products, arithmetic and copies ran while one was open for 0% of the time, Pallas kernels for 0%

commit v1 on v0

--- a/solution.py
+++ b/solution.py
@@ -1,7 +1,360 @@
+import functools
+
 import jax
 import jax.numpy as jnp
 from jax import lax
+from jax.experimental import pallas as pl
+from jax.experimental.pallas import tpu as pltpu
 from jax.sharding import PartitionSpec as P
+
+MESH = pl.DeviceIdType.MESH
+HIGH = lax.Precision.HIGHEST
+LAST = (((1,), (1,)), ((), ()))
+A_SUM, A_ALL, B_SUM, B_ALL, C_SUM, S_ALL, D_ALL, G_FRONT, G_LEAF, H_ALL = range(10)
+
+
+def fold(piece):
+    half = piece.shape[1] // 2
+    return jnp.concatenate([piece[:, :half], piece[:, half:]], axis=0)
+
+
+def unfold(piece):
+    piece = piece.astype(jnp.float32)
+    rows = piece.shape[0] // 2
+    return jnp.concatenate([piece[:rows], piece[rows:]], axis=1)
+
+
+def exact(left, right, dims=LAST):
+    return lax.dot_general(left, right, dims, precision=HIGH, preferred_element_type=jnp.float32)
+
+
+def fused(
+    leaves,
+    fronts,
+    live,
+    rhs_sub,
+    rhs_sep,
+    lower_inv,
+    upper_inv,
+    couple_low,
+    couple_up,
+    sep_lower,
+    sep_upper,
+    basis_sub,
+    basis_sep,
+    orth_sub,
+    orth_sep,
+    coef,
+    rhs_sub_v,
+    rhs_sep_v,
+    lower_v,
+    upper_v,
+    clow_v,
+    cup_v,
+    slow_v,
+    sup_v,
+    bsub_v,
+    bsep_v,
+    low_v,
+    sol_v,
+    a_send,
+    a_recv,
+    t_buf,
+    b_send,
+    b_recv,
+    l_buf,
+    c_send,
+    c_recv,
+    s_buf,
+    d_buf,
+    g_front,
+    g_leaf,
+    h_buf,
+    load,
+    send,
+    recv,
+):
+    leaf, front = lax.axis_index("leaf"), lax.axis_index("front")
+    count = leaves * fronts
+    me = leaf * fronts + front
+    blocks, size, _ = lower_v.shape
+    border = clow_v.shape[0]
+    width = s_buf.shape[2]
+    basis = bsub_v.shape[0]
+
+    def fetch(source, target, slot):
+        return pltpu.make_async_copy(source, target, load.at[slot])
+
+    def push(source, target, step, device):
+        pltpu.make_async_remote_copy(
+            src_ref=source,
+            dst_ref=target,
+            send_sem=send.at[step],
+            recv_sem=recv.at[step],
+            device_id=device,
+            device_id_type=MESH,
+        ).start()
+
+    def drain(view, sem):
+        pltpu.make_async_copy(view, view, sem).wait()
+
+    def device(k):
+        other = lax.rem(me + k, count)
+        return other // fronts, lax.rem(other, fronts)
+
+    def columns(index):
+        return pl.ds(pl.multiple_of(index * width, width), width)
+
+    first = [
+        fetch(rhs_sub, rhs_sub_v, 0),
+        fetch(lower_inv.at[pl.ds(0, 1)], lower_v.at[pl.ds(0, 1)], 1),
+        fetch(couple_low, clow_v, 2),
+    ]
+    second = [
+        fetch(rhs_sep, rhs_sep_v, 3),
+        fetch(lower_inv.at[pl.ds(1, blocks - 1)], lower_v.at[pl.ds(1, blocks - 1)], 4),
+        fetch(upper_inv, upper_v, 5),
+        fetch(basis_sub, bsub_v, 6),
+        fetch(basis_sep, bsep_v, 7),
+    ]
+    third = [fetch(sep_lower, slow_v, 8), fetch(sep_upper, sup_v, 9), fetch(couple_up, cup_v, 10)]
+    for copy in first:
+        copy.start()
+
+    barrier = pltpu.get_barrier_semaphore()
+
+    def greet(k, carry):
+        pl.semaphore_signal(barrier, inc=1, device_id=device(k), device_id_type=MESH)
+        return carry
+
+    lax.fori_loop(1, count, greet, 0)
+    for copy in second:
+        copy.start()
+
+    def live_part(value, k):
+        row = lax.broadcasted_iota(jnp.int32, value.shape, 1) + k * size
+        return jnp.where(row < live[0], value, 0.0)
+
+    def lower_block(k):
+        part = rhs_sub_v[:, k * size : (k + 1) * size].astype(jnp.bfloat16)
+        return live_part(jnp.dot(part, lower_v[k], preferred_element_type=jnp.float32), k)
+
+    def upper_block(value, k):
+        part = value.astype(jnp.bfloat16)
+        return live_part(jnp.dot(part, upper_v[k], preferred_element_type=jnp.float32), k)
+
+    first[0].wait()
+    first[1].wait()
+    low_v[...] = lower_block(0)
+    border_rows = low_v[:, :border].astype(jnp.bfloat16)
+    first[2].wait()
+    for copy in third:
+        copy.start()
+    pl.semaphore_wait(barrier, count - 1)
+
+    def couple(index):
+        return jnp.dot(border_rows, clow_v[:, columns(index)], preferred_element_type=jnp.float32)
+
+    def a_step(k, carry):
+        a_send[k - 1] = fold(couple(lax.rem(me + k, count))).astype(jnp.bfloat16)
+        push(a_send.at[k - 1], a_recv.at[k - 1], A_SUM, device(k))
+        return carry
+
+    lax.fori_loop(1, count, a_step, 0)
+
+    second[3].wait()
+    second[4].wait()
+    own = bsep_v[:, columns(front)]
+    gram = exact(bsub_v[...], bsub_v[...]) + exact(own, own)
+    g_front[front] = jnp.zeros(g_front.shape[1:], jnp.float32)
+    g_front[front, :, 0:basis] = gram
+    for k in range(1, fronts):
+        push(g_front.at[front], g_front.at[front], G_FRONT, (leaf, lax.rem(front + k, fronts)))
+    second[1].wait()
+    second[2].wait()
+    for k in range(1, blocks):
+        sol_v[:, k * size : (k + 1) * size] = upper_block(lower_block(k), k)
+    early = exact(sol_v[:, size:], bsub_v[:, size:])
+    second[0].wait()
+    top = rhs_sep_v[:, columns(front)] - couple(me)
+
+    drain(a_recv, recv.at[A_SUM])
+    top = fold(top) - jnp.sum(a_recv[...].astype(jnp.float32), axis=0)
+    t_buf[front] = top.astype(jnp.bfloat16)
+    for k in range(1, fronts):
+        push(t_buf.at[front], t_buf.at[front], A_ALL, (leaf, lax.rem(front + k, fronts)))
+
+    drain(g_front.at[pl.ds(0, fronts - 1)], recv.at[G_FRONT])
+    g_leaf[leaf] = jnp.sum(g_front[...], axis=0)
+    for k in range(1, leaves):
+        push(g_leaf.at[leaf], g_leaf.at[leaf], G_LEAF, (lax.rem(leaf + k, leaves), front))
+
+    third[0].wait()
+    drain(t_buf.at[pl.ds(0, fronts - 1)], recv.at[A_ALL])
+    rows = jnp.concatenate([unfold(t_buf[k]) for k in range(fronts)], axis=1).astype(jnp.bfloat16)
+
+    def lower_piece(index):
+        return jnp.dot(rows, slow_v[:, columns(index)], preferred_element_type=jnp.float32)
+
+    def b_step(k, carry):
+        to = lax.rem(leaf + k, leaves)
+        b_send[k - 1] = lower_piece(to)
+        push(b_send.at[k - 1], b_recv.at[k - 1], B_SUM, (to, front))
+        return carry
+
+    lax.fori_loop(1, leaves, b_step, 0)
+    piece = lower_piece(leaf)
+    drain(b_recv, recv.at[B_SUM])
+    piece = piece + jnp.sum(b_recv[...], axis=0)
+    l_buf[leaf] = fold(piece).astype(jnp.bfloat16)
+    for k in range(1, leaves):
+        push(l_buf.at[leaf], l_buf.at[leaf], B_ALL, (lax.rem(leaf + k, leaves), front))
+    third[1].wait()
+    drain(l_buf.at[pl.ds(0, leaves - 1)], recv.at[B_ALL])
+    rows2 = jnp.concatenate([unfold(l_buf[k]) for k in range(leaves)], axis=1).astype(jnp.bfloat16)
+
+    def upper_piece(index):
+        part = sup_v[pl.ds(pl.multiple_of(index * width, width), width), :]
+        return lax.dot_general(rows2, part, LAST, preferred_element_type=jnp.float32)
+
+    def c_step(k, carry):
+        to = lax.rem(front + k, fronts)
+        c_send[k - 1] = upper_piece(to)
+        push(c_send.at[k - 1], c_recv.at[k - 1], C_SUM, (leaf, to))
+        return carry
+
+    lax.fori_loop(1, fronts, c_step, 0)
+    piece = upper_piece(front)
+    drain(c_recv, recv.at[C_SUM])
+    piece = piece + jnp.sum(c_recv[...], axis=0)
+    d_buf[me] = fold(piece).astype(jnp.bfloat16)
+
+    def d_step(k, carry):
+        push(d_buf.at[me], d_buf.at[me], D_ALL, device(k))
+        return carry
+
+    lax.fori_loop(1, count, d_step, 0)
+    s_buf[front] = piece
+    for k in range(1, fronts):
+        push(s_buf.at[front], s_buf.at[front], S_ALL, (leaf, lax.rem(front + k, fronts)))
+    early = early + exact(piece, bsep_v[:, columns(front)])
+    third[2].wait()
+
+    drain(d_buf.at[pl.ds(0, count - 1)], recv.at[D_ALL])
+
+    def correct(k, total):
+        part = unfold(d_buf[k]).astype(jnp.bfloat16)
+        return total + lax.dot_general(
+            part, cup_v[:, columns(k)], LAST, preferred_element_type=jnp.float32
+        )
+
+    correction = lax.fori_loop(
+        0, count, correct, jnp.zeros((low_v.shape[0], border), jnp.float32), unroll=4
+    )
+    low_v[:, 0:border] = low_v[:, 0:border] - correction
+    sol_v[:, 0:size] = upper_block(low_v[...], 0)
+    h_buf[me] = jnp.zeros(h_buf.shape[1:], jnp.float32)
+    h_buf[me, :, 0:basis] = early + exact(sol_v[:, 0:size], bsub_v[:, 0:size])
+
+    def h_step(k, carry):
+        push(h_buf.at[me], h_buf.at[me], H_ALL, device(k))
+        return carry
+
+    lax.fori_loop(1, count, h_step, 0)
+    drain(g_leaf.at[pl.ds(0, leaves - 1)], recv.at[G_LEAF])
+    gram = jnp.sum(g_leaf[...], axis=0)[:, 0:basis]
+    drain(s_buf.at[pl.ds(0, fronts - 1)], recv.at[S_ALL])
+    drain(h_buf.at[pl.ds(0, count - 1)], recv.at[H_ALL])
+
+    once = jnp.sum(h_buf[...], axis=0)[:, 0:basis]
+    rows_cols = (((1,), (0,)), ((), ()))
+    both = once + (once - exact(once, gram, rows_cols))
+    coef[...] = both
+    orth_sub[...] = sol_v[...] - exact(both, bsub_v[...], rows_cols)
+    top_sol = jnp.concatenate([s_buf[k] for k in range(fronts)], axis=1)
+    orth_sep[...] = top_sol - exact(both, bsep_v[...], rows_cols)
+
+    drain(a_recv, send.at[A_SUM])
+    drain(t_buf.at[pl.ds(0, fronts - 1)], send.at[A_ALL])
+    drain(b_recv, send.at[B_SUM])
+    drain(l_buf.at[pl.ds(0, leaves - 1)], send.at[B_ALL])
+    drain(c_recv, send.at[C_SUM])
+    drain(s_buf.at[pl.ds(0, fronts - 1)], send.at[S_ALL])
+    drain(d_buf.at[pl.ds(0, count - 1)], send.at[D_ALL])
+    drain(g_front.at[pl.ds(0, fronts - 1)], send.at[G_FRONT])
+    drain(g_leaf.at[pl.ds(0, leaves - 1)], send.at[G_LEAF])
+    drain(h_buf.at[pl.ds(0, count - 1)], send.at[H_ALL])
+
+
+def fused_shards(
+    leaves,
+    fronts,
+    rhs_sub,
+    rhs_sep,
+    live_rows,
+    lower_inv,
+    upper_inv,
+    couple_low,
+    couple_up,
+    sep_lower_inv,
+    sep_upper_inv,
+    basis_sub,
+    basis_sep,
+):
+    vecs, basis = rhs_sub.shape[0], basis_sub.shape[0]
+    count = leaves * fronts
+    width = rhs_sep.shape[1] // fronts
+    size = lower_inv.shape[1]
+    full = [
+        rhs_sub, rhs_sep, lower_inv, upper_inv, couple_low, couple_up,
+        sep_lower_inv, sep_upper_inv, basis_sub, basis_sep,
+    ]
+    lanes = -(-basis // 128) * 128
+    narrow = (2 * vecs, width // 2)
+
+    def wide(*shape):
+        return pltpu.VMEM(shape, jnp.float32)
+
+    def slim(slots):
+        return pltpu.VMEM((slots,) + narrow, jnp.bfloat16)
+
+    vmem = pl.BlockSpec(memory_space=pltpu.VMEM)
+    orth_sub, orth_sep, coef = pl.pallas_call(
+        functools.partial(fused, leaves, fronts),
+        out_shape=(
+            jax.ShapeDtypeStruct(rhs_sub.shape, jnp.float32),
+            jax.ShapeDtypeStruct(rhs_sep.shape, jnp.float32),
+            jax.ShapeDtypeStruct((vecs, basis), jnp.float32),
+        ),
+        in_specs=[pl.BlockSpec(memory_space=pltpu.SMEM)]
+        + [pl.BlockSpec(memory_space=pl.ANY)] * len(full),
+        out_specs=(vmem, vmem, vmem),
+        scratch_shapes=[pltpu.VMEM(x.shape, x.dtype) for x in full]
+        + [
+            wide(vecs, size),
+            wide(*rhs_sub.shape),
+            slim(count - 1),
+            slim(count - 1),
+            slim(fronts),
+            wide(leaves - 1, vecs, width),
+            wide(leaves - 1, vecs, width),
+            slim(leaves),
+            wide(fronts - 1, vecs, width),
+            wide(fronts - 1, vecs, width),
+            wide(fronts, vecs, width),
+            slim(count),
+            wide(fronts, basis, lanes),
+            wide(leaves, basis, lanes),
+            wide(count, vecs, lanes),
+            pltpu.SemaphoreType.DMA((11,)),
+            pltpu.SemaphoreType.DMA((10,)),
+            pltpu.SemaphoreType.DMA((10,)),
+        ],
+        compiler_params=pltpu.CompilerParams(
+            collective_id=0, has_side_effects=True, vmem_limit_bytes=56 * 1024 * 1024
+        ),
+    )(live_rows, *full)
+    return orth_sub, orth_sep, coef.T
 
 
 def apply_blocks(vectors, inverse):
@@ -81,8 +434,16 @@
 
 
 def solution(mesh):
+    leaves, fronts = mesh.shape["leaf"], mesh.shape["front"]
+
+    def local(*arrays):
+        piece = arrays[1].shape[1] // fronts
+        if leaves > 1 and fronts > 1 and piece % 256 == 0 and arrays[0].shape[0] == 8:
+            return fused_shards(leaves, fronts, *arrays)
+        return shards(*arrays)
+
     return jax.shard_map(
-        shards,
+        local,
         mesh=mesh,
         in_specs=(
             P(None, ("leaf", "front")),

time: 360 us -> 59.3 us (0.16)
  blocking collectives: 186 us -> 0 us
  waiting for transfers between devices: 125 us -> 0 us
  Pallas kernels: 0 us -> 53.5 us
  matrix products: 31.1 us -> 0 us
  between operations: 14.6 us -> 1.29 us
  local copies, waits for them, and re-layouts: 0.1 us -> 4.22 us
    psum x5 -> x0, blocking collectives: 155 us -> none  [the longest x2 75.4 us: shards(): lax.psum(local_sub, ('leaf', 'front')) + lax.psum(local_sep, 'leaf')]
    reduce_scatter x1 -> x0, waiting for transfers between devices: 65.2 us -> none  [shards(): lax.psum_scatter(lax.dot_general(columns, border_rows, (((0,), (1,)), (()...]
    psum x2 -> x0, waiting for transfers between devices: 59.9 us -> none  [the longest x1 32.4 us: shards(): top_block = lax.psum(top_block, 'front')]
    pallas_call x0 -> x1, Pallas kernels: none -> 53.5 us  [fused_shards(): pl.pallas_call(functools.partial(fused, leaves, fronts), out_shape=(jax.S...]
    dot_general x14 -> x0, matrix products: 31.1 us -> none  [the longest x1 10.8 us: shards(): lax.dot_general(top_lower.astype(jnp.bfloat16), sep_upper_inv, (((1,), (1...]
    all_gather x1 -> x0, blocking collectives: 30.8 us -> none  [shards(): lax.all_gather(top_sol.astype(jnp.bfloat16), 'leaf', axis=1, tiled=True)]
    unnamed x6 -> x3, local copies, waits for them, and re-layouts: 0.02 us -> 4.22 us
  transfers between devices with their start and end apart: 3 -> 0, of which waited for: 3 -> 0; matrix products, arithmetic and copies ran while one was open for 0% -> 0% of each run, Pallas kernels for 0% -> 0%
where the time goes in v1:
time: 59.3 us; the launch traced here: 59 us
  Pallas kernels  53.5 us (90%)
  local copies, waits for them, and re-layouts  4.22 us (7%)
  between operations  1.29 us (2%)
    pallas_call x1, Pallas kernels, fused_shards(): pl.pallas_call(functools.partial(fused, leaves, fronts), out_shape=(jax.S...  53.5 us
    unnamed x3, local copies, waits for them, and re-layouts  4.22 us

profile of v1, /device:TPU:0, one launch (start us, length us, event | category | flops | bytes accessed | tf_op | source)
XLA Modules:
  0.0 59.0 jit_solution(4389880365055078468)
XLA Ops:
  1.3 53.5 %shard_map.130 = (f32[8,2048]{1,0:T(8,128)}, f32[8,2048]{1,0:T(8,128)}, f32[8,48]{1,0:T(8,128)}) custom-call(s32[1]{0:T(128)S(6)} %copy.17.live, f32[8,2048]{1,0:T(8,128)} %rhs_sub.1, f32[8,2048]{1,0:T(8,128)} %rhs_sep.1, bf16[8,256,256]{2,1,0:T(8,128)(2,1)} %lower_inv.1, bf16[8,256,256]{2,1,0:T(8,128)(2,1)} %upper_inv.1, bf16[64,16384]{1,0:T(8,128)(2,1)} %couple_low.1, ...), custom_call_target="tpu_custom_call" | custom-call | tf_op jit(solution)/shard_map/pallas_call | solution.py:322
  54.8 1.5 %copy.18 = f32[8,2048]{1,0:T(8,128)} copy(f32[8,2048]{1,0:T(8,128)} %get-tuple-element.12) | data formatting | bytes 131072
  56.3 1.5 %copy.19 = f32[8,2048]{1,0:T(8,128)} copy(f32[8,2048]{1,0:T(8,128)} %get-tuple-element.13) | data formatting | bytes 131072
  57.8 1.3 %copy.20 = f32[48,8]{0,1:T(8,128)} copy(f32[48,8]{0,1:T(8,128)} %bitcast.1) | data formatting | bytes 3072

commit v2 on v1

--- a/solution.py
+++ b/solution.py
@@ -10,7 +10,8 @@
 MESH = pl.DeviceIdType.MESH
 HIGH = lax.Precision.HIGHEST
 LAST = (((1,), (1,)), ((), ()))
-A_SUM, A_ALL, B_SUM, B_ALL, C_SUM, S_ALL, D_ALL, G_FRONT, G_LEAF, H_ALL = range(10)
+A_PAIR, A_SUM, A_ALL, B_SUM, B_ALL, C_SUM, S_ALL = range(7)
+D_ALL, D_PAIR, G_FRONT, G_LEAF, H_FRONT, H_LEAF = range(7, 13)
 
 
 def fold(piece):
@@ -26,6 +27,30 @@
 
 def exact(left, right, dims=LAST):
     return lax.dot_general(left, right, dims, precision=HIGH, preferred_element_type=jnp.float32)
+
+
+def flip(index, k):
+    bit, result = 1, index
+    while bit <= k:
+        if k & bit:
+            result = result + bit * (1 - 2 * lax.rem(index // bit, 2))
+        bit *= 2
+    return result
+
+
+def hand_over(sub, sep, products, orth_sub, orth_sep, coef, held, sems):
+    copies = [
+        pltpu.make_async_copy(source, target, sems.at[slot])
+        for slot, (source, target) in enumerate(
+            [(products, held), (sub, orth_sub), (sep, orth_sep)]
+        )
+    ]
+    for copy in copies:
+        copy.start()
+    copies[0].wait()
+    coef[...] = jnp.transpose(held[...])[: coef.shape[0]]
+    copies[1].wait()
+    copies[2].wait()
 
 
 def fused(
@@ -57,26 +82,35 @@
     bsep_v,
     low_v,
     sol_v,
+    a_part,
+    a_pair,
     a_send,
     a_recv,
     t_buf,
+    b_acc,
     b_send,
     b_recv,
     l_buf,
+    c_acc,
     c_send,
     c_recv,
     s_buf,
     d_buf,
     g_front,
     g_leaf,
-    h_buf,
+    h_front,
+    h_leaf,
     load,
     send,
     recv,
+    recv_pair,
+    recv_front,
+    recv_leaf,
 ):
     leaf, front = lax.axis_index("leaf"), lax.axis_index("front")
-    count = leaves * fronts
-    me = leaf * fronts + front
+    half, per_leaf = leaves * fronts // 2, fronts // 2
+    parity, place = lax.rem(front, 2), leaf * per_leaf + front // 2
+    mate = (leaf, flip(front, 1))
     blocks, size, _ = lower_v.shape
     border = clow_v.shape[0]
     width = s_buf.shape[2]
@@ -85,12 +119,12 @@
     def fetch(source, target, slot):
         return pltpu.make_async_copy(source, target, load.at[slot])
 
-    def push(source, target, step, device):
+    def push(source, target, step, device, arrived=None):
         pltpu.make_async_remote_copy(
             src_ref=source,
             dst_ref=target,
             send_sem=send.at[step],
-            recv_sem=recv.at[step],
+            recv_sem=recv.at[step] if arrived is None else arrived,
             device_id=device,
             device_id_type=MESH,
         ).start()
@@ -99,8 +133,8 @@
         pltpu.make_async_copy(view, view, sem).wait()
 
     def device(k):
-        other = lax.rem(me + k, count)
-        return other // fronts, lax.rem(other, fronts)
+        other = lax.rem(place + k, half)
+        return other // per_leaf, 2 * lax.rem(other, per_leaf) + parity
 
     def columns(index):
         return pl.ds(pl.multiple_of(index * width, width), width)
@@ -127,7 +161,11 @@
         pl.semaphore_signal(barrier, inc=1, device_id=device(k), device_id_type=MESH)
         return carry
 
-    lax.fori_loop(1, count, greet, 0)
+    lax.fori_loop(1, half, greet, 0)
+    for k in range(1, fronts, 2):
+        pl.semaphore_signal(
+            barrier, inc=1, device_id=(leaf, flip(front, k)), device_id_type=MESH
+        )
     for copy in second:
         copy.start()
 
@@ -150,17 +188,38 @@
     first[2].wait()
     for copy in third:
         copy.start()
-    pl.semaphore_wait(barrier, count - 1)
-
-    def couple(index):
-        return jnp.dot(border_rows, clow_v[:, columns(index)], preferred_element_type=jnp.float32)
+
+    greeted = False
+    for group in range(2):
+        ahead, some = group * (half // 2), half // 2
+        for q in range(ahead, ahead + some):
+            for p in range(2):
+                at = (2 * q + p) * width
+                a_part[p, q] = jnp.dot(
+                    border_rows, clow_v[:, at : at + width], preferred_element_type=jnp.float32
+                )
+        if not greeted:
+            pl.semaphore_wait(barrier, half - 1 + fronts // 2)
+            greeted = True
+        push(
+            a_part.at[1 - parity, pl.ds(ahead, some)],
+            a_pair.at[pl.ds(ahead, some)],
+            A_PAIR,
+            mate,
+            recv_pair.at[group],
+        )
+    second[0].wait()
+    for group in range(2):
+        ahead, some = group * (half // 2), half // 2
+        drain(a_pair.at[pl.ds(ahead, some)], recv_pair.at[group])
+        for q in range(ahead, ahead + some):
+            a_send[q] = fold(a_part[parity, q] + a_pair[q]).astype(jnp.bfloat16)
 
     def a_step(k, carry):
-        a_send[k - 1] = fold(couple(lax.rem(me + k, count))).astype(jnp.bfloat16)
-        push(a_send.at[k - 1], a_recv.at[k - 1], A_SUM, device(k))
+        push(a_send.at[lax.rem(place + k, half)], a_recv.at[k - 1], A_SUM, device(k))
         return carry
 
-    lax.fori_loop(1, count, a_step, 0)
+    lax.fori_loop(1, half, a_step, 0)
 
     second[3].wait()
     second[4].wait()
@@ -169,121 +228,154 @@
     g_front[front] = jnp.zeros(g_front.shape[1:], jnp.float32)
     g_front[front, :, 0:basis] = gram
     for k in range(1, fronts):
-        push(g_front.at[front], g_front.at[front], G_FRONT, (leaf, lax.rem(front + k, fronts)))
+        push(g_front.at[front], g_front.at[front], G_FRONT, (leaf, flip(front, k)))
+    top = rhs_sep_v[:, columns(front)] - (a_part[parity, place] + a_pair[place])
+
+    drain(a_recv, recv.at[A_SUM])
+    top = fold(top) - jnp.sum(a_recv[...].astype(jnp.float32), axis=0)
+    t_buf[0] = top.astype(jnp.bfloat16)
+    for k in range(fronts - 1, 0, -1):
+        push(t_buf.at[0], t_buf.at[k], A_ALL, (leaf, flip(front, k)), recv_front.at[k])
+
+    def strip(index):
+        return pl.ds(pl.multiple_of(index * width, width), width)
+
+    def top_piece(k):
+        if k:
+            drain(t_buf.at[k], recv_front.at[k])
+        return unfold(t_buf[k]).astype(jnp.bfloat16), strip(flip(front, k))
+
+    def times_lower(piece, to):
+        return jnp.dot(piece[0], slow_v[piece[1], to], preferred_element_type=jnp.float32)
+
+    third[0].wait()
+    for k in range(fronts - 2):
+        piece = top_piece(k)
+        for n in range(leaves):
+            product = times_lower(piece, slice(n * width, (n + 1) * width))
+            b_acc[n] = b_acc[n] + product if k else product
+        if k == 0:
+            drain(g_front.at[pl.ds(0, fronts - 1)], recv.at[G_FRONT])
+            g_leaf[leaf] = jnp.sum(g_front[...], axis=0)
+            for j in range(1, leaves):
+                push(g_leaf.at[leaf], g_leaf.at[leaf], G_LEAF, (flip(leaf, j), front))
+    last = [top_piece(k) for k in range(fronts - 2, fronts)]
+
+    def lower_piece(to):
+        return b_acc[to] + sum(times_lower(piece, columns(to)) for piece in last)
+
+    for k in range(leaves - 1, 0, -1):
+        to = flip(leaf, k)
+        b_send[k - 1] = lower_piece(to)
+        push(b_send.at[k - 1], b_recv.at[k - 1], B_SUM, (to, front))
+    piece = lower_piece(leaf)
+    drain(b_recv, recv.at[B_SUM])
+    piece = piece + jnp.sum(b_recv[...], axis=0)
+    l_buf[0] = fold(piece).astype(jnp.bfloat16)
+    for k in range(leaves - 1, 0, -1):
+        push(l_buf.at[0], l_buf.at[k], B_ALL, (flip(leaf, k), front), recv_leaf.at[k])
+
+    def low_piece(k):
+        if k:
+            drain(l_buf.at[k], recv_leaf.at[k])
+        return unfold(l_buf[k]).astype(jnp.bfloat16), columns(flip(leaf, k))
+
+    def times_upper(piece, to):
+        return lax.dot_general(
+            piece[0], sup_v[to, piece[1]], LAST, preferred_element_type=jnp.float32
+        )
+
+    third[1].wait()
+    for k in range(leaves - 2):
+        piece = low_piece(k)
+        for n in range(fronts):
+            product = times_upper(piece, slice(n * width, (n + 1) * width))
+            c_acc[n] = c_acc[n] + product if k else product
+    last2 = [low_piece(k) for k in range(leaves - 2, leaves)]
+
+    def upper_piece(to):
+        return c_acc[to] + sum(times_upper(piece, strip(to)) for piece in last2)
+
+    for k in range(fronts - 1, 0, -1):
+        to = flip(front, k)
+        c_send[k - 1] = upper_piece(to)
+        push(c_send.at[k - 1], c_recv.at[k - 1], C_SUM, (leaf, to))
+    piece = upper_piece(front)
+    drain(c_recv, recv.at[C_SUM])
+    piece = piece + jnp.sum(c_recv[...], axis=0)
+
+    d_buf[parity, place] = fold(piece).astype(jnp.bfloat16)
+    mine = d_buf.at[parity, place]
+
+    def d_step(k, carry):
+        push(mine, mine, D_ALL, device(k))
+        return carry
+
+    lax.fori_loop(1, half, d_step, 0)
+    s_buf[front] = piece
+    for k in range(1, fronts):
+        push(s_buf.at[front], s_buf.at[front], S_ALL, (leaf, flip(front, k)))
+
     second[1].wait()
     second[2].wait()
     for k in range(1, blocks):
         sol_v[:, k * size : (k + 1) * size] = upper_block(lower_block(k), k)
-    early = exact(sol_v[:, size:], bsub_v[:, size:])
-    second[0].wait()
-    top = rhs_sep_v[:, columns(front)] - couple(me)
-
-    drain(a_recv, recv.at[A_SUM])
-    top = fold(top) - jnp.sum(a_recv[...].astype(jnp.float32), axis=0)
-    t_buf[front] = top.astype(jnp.bfloat16)
-    for k in range(1, fronts):
-        push(t_buf.at[front], t_buf.at[front], A_ALL, (leaf, lax.rem(front + k, fronts)))
-
-    drain(g_front.at[pl.ds(0, fronts - 1)], recv.at[G_FRONT])
-    g_leaf[leaf] = jnp.sum(g_front[...], axis=0)
-    for k in range(1, leaves):
-        push(g_leaf.at[leaf], g_leaf.at[leaf], G_LEAF, (lax.rem(leaf + k, leaves), front))
-
-    third[0].wait()
-    drain(t_buf.at[pl.ds(0, fronts - 1)], recv.at[A_ALL])
-    rows = jnp.concatenate([unfold(t_buf[k]) for k in range(fronts)], axis=1).astype(jnp.bfloat16)
-
-    def lower_piece(index):
-        return jnp.dot(rows, slow_v[:, columns(index)], preferred_element_type=jnp.float32)
-
-    def b_step(k, carry):
-        to = lax.rem(leaf + k, leaves)
-        b_send[k - 1] = lower_piece(to)
-        push(b_send.at[k - 1], b_recv.at[k - 1], B_SUM, (to, front))
-        return carry
-
-    lax.fori_loop(1, leaves, b_step, 0)
-    piece = lower_piece(leaf)
-    drain(b_recv, recv.at[B_SUM])
-    piece = piece + jnp.sum(b_recv[...], axis=0)
-    l_buf[leaf] = fold(piece).astype(jnp.bfloat16)
-    for k in range(1, leaves):
-        push(l_buf.at[leaf], l_buf.at[leaf], B_ALL, (lax.rem(leaf + k, leaves), front))
-    third[1].wait()
-    drain(l_buf.at[pl.ds(0, leaves - 1)], recv.at[B_ALL])
-    rows2 = jnp.concatenate([unfold(l_buf[k]) for k in range(leaves)], axis=1).astype(jnp.bfloat16)
-
-    def upper_piece(index):
-        part = sup_v[pl.ds(pl.multiple_of(index * width, width), width), :]
-        return lax.dot_general(rows2, part, LAST, preferred_element_type=jnp.float32)
-
-    def c_step(k, carry):
-        to = lax.rem(front + k, fronts)
-        c_send[k - 1] = upper_piece(to)
-        push(c_send.at[k - 1], c_recv.at[k - 1], C_SUM, (leaf, to))
-        return carry
-
-    lax.fori_loop(1, fronts, c_step, 0)
-    piece = upper_piece(front)
-    drain(c_recv, recv.at[C_SUM])
-    piece = piece + jnp.sum(c_recv[...], axis=0)
-    d_buf[me] = fold(piece).astype(jnp.bfloat16)
-
-    def d_step(k, carry):
-        push(d_buf.at[me], d_buf.at[me], D_ALL, device(k))
-        return carry
-
-    lax.fori_loop(1, count, d_step, 0)
-    s_buf[front] = piece
-    for k in range(1, fronts):
-        push(s_buf.at[front], s_buf.at[front], S_ALL, (leaf, lax.rem(front + k, fronts)))
-    early = early + exact(piece, bsep_v[:, columns(front)])
+    early = exact(sol_v[:, size:], bsub_v[:, size:]) + exact(piece, bsep_v[:, columns(front)])
     third[2].wait()
 
-    drain(d_buf.at[pl.ds(0, count - 1)], recv.at[D_ALL])
-
-    def correct(k, total):
-        part = unfold(d_buf[k]).astype(jnp.bfloat16)
-        return total + lax.dot_general(
-            part, cup_v[:, columns(k)], LAST, preferred_element_type=jnp.float32
-        )
-
-    correction = lax.fori_loop(
-        0, count, correct, jnp.zeros((low_v.shape[0], border), jnp.float32), unroll=4
-    )
+    def correct(p):
+        return sum(
+            lax.dot_general(
+                unfold(d_buf[p, q]).astype(jnp.bfloat16),
+                cup_v[:, columns(2 * q + p)],
+                LAST,
+                preferred_element_type=jnp.float32,
+            )
+            for q in range(half)
+        )
+
+    drain(d_buf.at[0, pl.ds(0, half - 1)], recv.at[D_ALL])
+    push(d_buf.at[parity], d_buf.at[parity], D_PAIR, mate)
+    correction = correct(parity)
+    drain(d_buf.at[0], recv.at[D_PAIR])
+    correction = correction + correct(1 - parity)
     low_v[:, 0:border] = low_v[:, 0:border] - correction
     sol_v[:, 0:size] = upper_block(low_v[...], 0)
-    h_buf[me] = jnp.zeros(h_buf.shape[1:], jnp.float32)
-    h_buf[me, :, 0:basis] = early + exact(sol_v[:, 0:size], bsub_v[:, 0:size])
-
-    def h_step(k, carry):
-        push(h_buf.at[me], h_buf.at[me], H_ALL, device(k))
-        return carry
-
-    lax.fori_loop(1, count, h_step, 0)
+    h_front[front] = jnp.zeros(h_front.shape[1:], jnp.float32)
+    h_front[front, :, 0:basis] = early + exact(sol_v[:, 0:size], bsub_v[:, 0:size])
+    for k in range(fronts - 1, 0, -1):
+        push(h_front.at[front], h_front.at[front], H_FRONT, (leaf, flip(front, k)))
     drain(g_leaf.at[pl.ds(0, leaves - 1)], recv.at[G_LEAF])
     gram = jnp.sum(g_leaf[...], axis=0)[:, 0:basis]
+    drain(h_front.at[pl.ds(0, fronts - 1)], recv.at[H_FRONT])
+    h_leaf[leaf] = jnp.sum(h_front[...], axis=0)
+    for k in range(leaves - 1, 0, -1):
+        push(h_leaf.at[leaf], h_leaf.at[leaf], H_LEAF, (flip(leaf, k), front))
     drain(s_buf.at[pl.ds(0, fronts - 1)], recv.at[S_ALL])
-    drain(h_buf.at[pl.ds(0, count - 1)], recv.at[H_ALL])
-
-    once = jnp.sum(h_buf[...], axis=0)[:, 0:basis]
+    drain(h_leaf.at[pl.ds(0, leaves - 1)], recv.at[H_LEAF])
+
+    once = jnp.sum(h_leaf[...], axis=0)[:, 0:basis]
     rows_cols = (((1,), (0,)), ((), ()))
     both = once + (once - exact(once, gram, rows_cols))
-    coef[...] = both
+    coef[...] = jnp.zeros(coef.shape, jnp.float32)
+    coef[:, 0:basis] = both
     orth_sub[...] = sol_v[...] - exact(both, bsub_v[...], rows_cols)
     top_sol = jnp.concatenate([s_buf[k] for k in range(fronts)], axis=1)
     orth_sep[...] = top_sol - exact(both, bsep_v[...], rows_cols)
 
+    drain(a_pair, send.at[A_PAIR])
     drain(a_recv, send.at[A_SUM])
     drain(t_buf.at[pl.ds(0, fronts - 1)], send.at[A_ALL])
     drain(b_recv, send.at[B_SUM])
     drain(l_buf.at[pl.ds(0, leaves - 1)], send.at[B_ALL])
     drain(c_recv, send.at[C_SUM])
     drain(s_buf.at[pl.ds(0, fronts - 1)], send.at[S_ALL])
-    drain(d_buf.at[pl.ds(0, count - 1)], send.at[D_ALL])
+    drain(d_buf.at[0, pl.ds(0, half - 1)], send.at[D_ALL])
+    drain(d_buf.at[0], send.at[D_PAIR])
     drain(g_front.at[pl.ds(0, fronts - 1)], send.at[G_FRONT])
     drain(g_leaf.at[pl.ds(0, leaves - 1)], send.at[G_LEAF])
-    drain(h_buf.at[pl.ds(0, count - 1)], send.at[H_ALL])
+    drain(h_front.at[pl.ds(0, fronts - 1)], send.at[H_FRONT])
+    drain(h_leaf.at[pl.ds(0, leaves - 1)], send.at[H_LEAF])
 
 
 def fused_shards(
@@ -302,7 +394,7 @@
     basis_sep,
 ):
     vecs, basis = rhs_sub.shape[0], basis_sub.shape[0]
-    count = leaves * fronts
+    half = leaves * fronts // 2
     width = rhs_sep.shape[1] // fronts
     size = lower_inv.shape[1]
     full = [
@@ -319,12 +411,13 @@
         return pltpu.VMEM((slots,) + narrow, jnp.bfloat16)
 
     vmem = pl.BlockSpec(memory_space=pltpu.VMEM)
-    orth_sub, orth_sep, coef = pl.pallas_call(
+    anywhere = pl.BlockSpec(memory_space=pl.ANY)
+    parts = pl.pallas_call(
         functools.partial(fused, leaves, fronts),
         out_shape=(
             jax.ShapeDtypeStruct(rhs_sub.shape, jnp.float32),
             jax.ShapeDtypeStruct(rhs_sep.shape, jnp.float32),
-            jax.ShapeDtypeStruct((vecs, basis), jnp.float32),
+            jax.ShapeDtypeStruct((vecs, lanes), jnp.float32),
         ),
         in_specs=[pl.BlockSpec(memory_space=pltpu.SMEM)]
         + [pl.BlockSpec(memory_space=pl.ANY)] * len(full),
@@ -333,28 +426,47 @@
         + [
             wide(vecs, size),
             wide(*rhs_sub.shape),
-            slim(count - 1),
-            slim(count - 1),
+            wide(2, half, vecs, width),
+            wide(half, vecs, width),
+            slim(half),
+            slim(half - 1),
             slim(fronts),
+            wide(leaves, vecs, width),
             wide(leaves - 1, vecs, width),
             wide(leaves - 1, vecs, width),
             slim(leaves),
+            wide(fronts, vecs, width),
             wide(fronts - 1, vecs, width),
             wide(fronts - 1, vecs, width),
             wide(fronts, vecs, width),
-            slim(count),
+            pltpu.VMEM((2, half) + narrow, jnp.bfloat16),
             wide(fronts, basis, lanes),
             wide(leaves, basis, lanes),
-            wide(count, vecs, lanes),
+            wide(fronts, vecs, lanes),
+            wide(leaves, vecs, lanes),
             pltpu.SemaphoreType.DMA((11,)),
-            pltpu.SemaphoreType.DMA((10,)),
-            pltpu.SemaphoreType.DMA((10,)),
+            pltpu.SemaphoreType.DMA((13,)),
+            pltpu.SemaphoreType.DMA((13,)),
+            pltpu.SemaphoreType.DMA((2,)),
+            pltpu.SemaphoreType.DMA((fronts,)),
+            pltpu.SemaphoreType.DMA((leaves,)),
         ],
         compiler_params=pltpu.CompilerParams(
             collective_id=0, has_side_effects=True, vmem_limit_bytes=56 * 1024 * 1024
         ),
     )(live_rows, *full)
-    return orth_sub, orth_sep, coef.T
+    return pl.pallas_call(
+        hand_over,
+        out_shape=(
+            jax.ShapeDtypeStruct(rhs_sub.shape, jnp.float32),
+            jax.ShapeDtypeStruct(rhs_sep.shape, jnp.float32),
+            jax.ShapeDtypeStruct((basis, vecs), jnp.float32),
+        ),
+        in_specs=[anywhere] * 3,
+        out_specs=(anywhere, anywhere, vmem),
+        scratch_shapes=[wide(vecs, lanes), pltpu.SemaphoreType.DMA((3,))],
+        compiler_params=pltpu.CompilerParams(vmem_limit_bytes=56 * 1024 * 1024),
+    )(*parts)
 
 
 def apply_blocks(vectors, inverse):
@@ -438,7 +550,8 @@
 
     def local(*arrays):
         piece = arrays[1].shape[1] // fronts
-        if leaves > 1 and fronts > 1 and piece % 256 == 0 and arrays[0].shape[0] == 8:
+        paired = leaves > 2 and fronts > 2 and not (leaves & (leaves - 1) or fronts & (fronts - 1))
+        if paired and piece % 256 == 0 and arrays[0].shape[0] == 8:
             return fused_shards(leaves, fronts, *arrays)
         return shards(*arrays)
 

time: 59.3 us -> 56.7 us (0.956)
  local copies, waits for them, and re-layouts: 4.22 us -> 1.4 us
    pallas_call x0 -> x1, Pallas kernels: none -> 5.7 us  [fused_shards(): pl.pallas_call(hand_over, out_shape=(jax.ShapeDtypeStruct(rhs_sub.shape,...]
    pallas_call x1, Pallas kernels: 53.5 us -> 48.1 us  [fused_shards(): pl.pallas_call(functools.partial(fused, leaves, fronts), out_shape=(jax.S...]
    unnamed x3 -> x0, local copies, waits for them, and re-layouts: 4.22 us -> none
    pallas_call x0 -> x1, local copies, waits for them, and re-layouts: none -> 1.4 us  [fused_shards(): pl.pallas_call(hand_over, out_shape=(jax.ShapeDtypeStruct(rhs_sub.shape,...]
where the time goes in v2:
time: 56.7 us; the launch traced here: 56.5 us
  Pallas kernels  53.8 us (95%)
  local copies, waits for them, and re-layouts  1.4 us (2%)
  between operations  1.3 us (2%)
    pallas_call x1, Pallas kernels, fused_shards(): pl.pallas_call(functools.partial(fused, leaves, fronts), out_shape=(jax.S...  48.1 us
    pallas_call x1, Pallas kernels, fused_shards(): pl.pallas_call(hand_over, out_shape=(jax.ShapeDtypeStruct(rhs_sub.shape,...  5.7 us
    pallas_call x1, local copies, waits for them, and re-layouts, fused_shards(): pl.pallas_call(hand_over, out_shape=(jax.ShapeDtypeStruct(rhs_sub.shape,...  1.4 us

profile of v2, /device:TPU:0, one launch (start us, length us, event | category | flops | bytes accessed | tf_op | source)
XLA Modules:
  0.0 56.5 jit_solution(4404864212424166114)
XLA Ops:
  1.3 48.1 %shard_map.130 = (f32[8,2048]{1,0:T(8,128)}, f32[8,2048]{1,0:T(8,128)}, f32[8,128]{1,0:T(8,128)}) custom-call(s32[1]{0:T(128)S(6)} %copy.15.live, f32[8,2048]{1,0:T(8,128)} %rhs_sub.1, f32[8,2048]{1,0:T(8,128)} %rhs_sep.1, bf16[8,256,256]{2,1,0:T(8,128)(2,1)} %lower_inv.1, bf16[8,256,256]{2,1,0:T(8,128)(2,1)} %upper_inv.1, bf16[64,16384]{1,0:T(8,128)(2,1)} %couple_low.1, ...), custom_call_target="tpu_custom_call" | custom-call | tf_op jit(solution)/shard_map/pallas_call | solution.py:415
  49.4 5.7 %shard_map.131 = (f32[8,2048]{1,0:T(8,128)}, f32[8,2048]{1,0:T(8,128)}, f32[48,8]{1,0:T(8,128)}) custom-call(f32[8,2048]{1,0:T(8,128)} %get-tuple-element.6.sub, f32[8,2048]{1,0:T(8,128)} %get-tuple-element.7.sep, f32[8,128]{1,0:T(8,128)} %get-tuple-element.8.products), custom_call_target="tpu_custom_call" | custom-call | tf_op jit(solution)/shard_map/pallas_call | solution.py:458
  55.1 1.4 %copy.14 = f32[48,8]{0,1:T(8,128)} copy(f32[48,8]{1,0:T(8,128)} %get-tuple-element.11) | data formatting | bytes 3072 | tf_op jit(solution)/shard_map/pallas_call | solution.py:458

commit v3 on v2

--- a/solution.py
+++ b/solution.py
@@ -38,25 +38,23 @@
     return result
 
 
-def hand_over(sub, sep, products, orth_sub, orth_sep, coef, held, sems):
-    copies = [
-        pltpu.make_async_copy(source, target, sems.at[slot])
-        for slot, (source, target) in enumerate(
-            [(products, held), (sub, orth_sub), (sep, orth_sep)]
-        )
-    ]
-    for copy in copies:
+def hand_over(*refs):
+    given, placed, held, (into, out) = refs[:3], refs[3:6], refs[6:9], refs[9:]
+    reads = [pltpu.make_async_copy(given[k], held[k], into.at[k]) for k in range(3)]
+    writes = [pltpu.make_async_copy(held[k], placed[k], out.at[k]) for k in range(3)]
+    for copy in reads:
         copy.start()
-    copies[0].wait()
-    coef[...] = jnp.transpose(held[...])[: coef.shape[0]]
-    copies[1].wait()
-    copies[2].wait()
+    for read, write in zip(reads, writes):
+        read.wait()
+        write.start()
+    for copy in writes:
+        copy.wait()
 
 
 def fused(
     leaves,
     fronts,
-    live,
+    live_rows,
     rhs_sub,
     rhs_sep,
     lower_inv,
@@ -106,6 +104,7 @@
     recv_pair,
     recv_front,
     recv_leaf,
+    live,
 ):
     leaf, front = lax.axis_index("leaf"), lax.axis_index("front")
     half, per_leaf = leaves * fronts // 2, fronts // 2
@@ -133,8 +132,7 @@
         pltpu.make_async_copy(view, view, sem).wait()
 
     def device(k):
-        other = lax.rem(place + k, half)
-        return other // per_leaf, 2 * lax.rem(other, per_leaf) + parity
+        return flip(leaf, k // per_leaf), flip(front, 2 * (k % per_leaf))
 
     def columns(index):
         return pl.ds(pl.multiple_of(index * width, width), width)
@@ -143,6 +141,7 @@
         fetch(rhs_sub, rhs_sub_v, 0),
         fetch(lower_inv.at[pl.ds(0, 1)], lower_v.at[pl.ds(0, 1)], 1),
         fetch(couple_low, clow_v, 2),
+        fetch(live_rows, live, 11),
     ]
     second = [
         fetch(rhs_sep, rhs_sep_v, 3),
@@ -151,17 +150,20 @@
         fetch(basis_sub, bsub_v, 6),
         fetch(basis_sep, bsep_v, 7),
     ]
-    third = [fetch(sep_lower, slow_v, 8), fetch(sep_upper, sup_v, 9), fetch(couple_up, cup_v, 10)]
+
+    def fetch_rows(source, target, slot):
+        rows = source.shape[0] // 4
+        for k in range(4):
+            some = pl.ds(k * rows, rows)
+            fetch(source.at[some], target.at[some], slot).start()
+
     for copy in first:
         copy.start()
 
     barrier = pltpu.get_barrier_semaphore()
 
-    def greet(k, carry):
+    for k in range(1, half):
         pl.semaphore_signal(barrier, inc=1, device_id=device(k), device_id_type=MESH)
-        return carry
-
-    lax.fori_loop(1, half, greet, 0)
     for k in range(1, fronts, 2):
         pl.semaphore_signal(
             barrier, inc=1, device_id=(leaf, flip(front, k)), device_id_type=MESH
@@ -183,11 +185,11 @@
 
     first[0].wait()
     first[1].wait()
+    first[3].wait()
     low_v[...] = lower_block(0)
     border_rows = low_v[:, :border].astype(jnp.bfloat16)
     first[2].wait()
-    for copy in third:
-        copy.start()
+    fetch_rows(sep_lower, slow_v, 8)
 
     greeted = False
     for group in range(2):
@@ -215,11 +217,8 @@
         for q in range(ahead, ahead + some):
             a_send[q] = fold(a_part[parity, q] + a_pair[q]).astype(jnp.bfloat16)
 
-    def a_step(k, carry):
-        push(a_send.at[lax.rem(place + k, half)], a_recv.at[k - 1], A_SUM, device(k))
-        return carry
-
-    lax.fori_loop(1, half, a_step, 0)
+    for k in range(half - 1, 0, -1):
+        push(a_send.at[flip(place, k)], a_recv.at[k - 1], A_SUM, device(k))
 
     second[3].wait()
     second[4].wait()
@@ -248,7 +247,9 @@
     def times_lower(piece, to):
         return jnp.dot(piece[0], slow_v[piece[1], to], preferred_element_type=jnp.float32)
 
-    third[0].wait()
+    drain(slow_v, load.at[8])
+    fetch_rows(sep_upper, sup_v, 9)
+    fetch(couple_up, cup_v, 10).start()
     for k in range(fronts - 2):
         piece = top_piece(k)
         for n in range(leaves):
@@ -285,7 +286,7 @@
             piece[0], sup_v[to, piece[1]], LAST, preferred_element_type=jnp.float32
         )
 
-    third[1].wait()
+    drain(sup_v, load.at[9])
     for k in range(leaves - 2):
         piece = low_piece(k)
         for n in range(fronts):
@@ -307,11 +308,8 @@
     d_buf[parity, place] = fold(piece).astype(jnp.bfloat16)
     mine = d_buf.at[parity, place]
 
-    def d_step(k, carry):
+    for k in range(half - 1, 0, -1):
         push(mine, mine, D_ALL, device(k))
-        return carry
-
-    lax.fori_loop(1, half, d_step, 0)
     s_buf[front] = piece
     for k in range(1, fronts):
         push(s_buf.at[front], s_buf.at[front], S_ALL, (leaf, flip(front, k)))
@@ -321,7 +319,7 @@
     for k in range(1, blocks):
         sol_v[:, k * size : (k + 1) * size] = upper_block(lower_block(k), k)
     early = exact(sol_v[:, size:], bsub_v[:, size:]) + exact(piece, bsep_v[:, columns(front)])
-    third[2].wait()
+    drain(cup_v, load.at[10])
 
     def correct(p):
         return sum(
@@ -357,8 +355,7 @@
     once = jnp.sum(h_leaf[...], axis=0)[:, 0:basis]
     rows_cols = (((1,), (0,)), ((), ()))
     both = once + (once - exact(once, gram, rows_cols))
-    coef[...] = jnp.zeros(coef.shape, jnp.float32)
-    coef[:, 0:basis] = both
+    coef[...] = both
     orth_sub[...] = sol_v[...] - exact(both, bsub_v[...], rows_cols)
     top_sol = jnp.concatenate([s_buf[k] for k in range(fronts)], axis=1)
     orth_sep[...] = top_sol - exact(both, bsep_v[...], rows_cols)
@@ -411,16 +408,15 @@
         return pltpu.VMEM((slots,) + narrow, jnp.bfloat16)
 
     vmem = pl.BlockSpec(memory_space=pltpu.VMEM)
-    anywhere = pl.BlockSpec(memory_space=pl.ANY)
+    anywhere = pl.BlockSpec(memory_space=pltpu.HBM)
     parts = pl.pallas_call(
         functools.partial(fused, leaves, fronts),
         out_shape=(
             jax.ShapeDtypeStruct(rhs_sub.shape, jnp.float32),
             jax.ShapeDtypeStruct(rhs_sep.shape, jnp.float32),
-            jax.ShapeDtypeStruct((vecs, lanes), jnp.float32),
+            jax.ShapeDtypeStruct((vecs, basis), jnp.float32),
         ),
-        in_specs=[pl.BlockSpec(memory_space=pltpu.SMEM)]
-        + [pl.BlockSpec(memory_space=pl.ANY)] * len(full),
+        in_specs=[anywhere] * (len(full) + 1),
         out_specs=(vmem, vmem, vmem),
         scratch_shapes=[pltpu.VMEM(x.shape, x.dtype) for x in full]
         + [
@@ -444,29 +440,28 @@
             wide(leaves, basis, lanes),
             wide(fronts, vecs, lanes),
             wide(leaves, vecs, lanes),
-            pltpu.SemaphoreType.DMA((11,)),
+            pltpu.SemaphoreType.DMA((12,)),
             pltpu.SemaphoreType.DMA((13,)),
             pltpu.SemaphoreType.DMA((13,)),
             pltpu.SemaphoreType.DMA((2,)),
             pltpu.SemaphoreType.DMA((fronts,)),
             pltpu.SemaphoreType.DMA((leaves,)),
+            pltpu.SMEM(live_rows.shape, jnp.int32),
         ],
         compiler_params=pltpu.CompilerParams(
             collective_id=0, has_side_effects=True, vmem_limit_bytes=56 * 1024 * 1024
         ),
     )(live_rows, *full)
-    return pl.pallas_call(
+    orth_sub, orth_sep, coef = pl.pallas_call(
         hand_over,
-        out_shape=(
-            jax.ShapeDtypeStruct(rhs_sub.shape, jnp.float32),
-            jax.ShapeDtypeStruct(rhs_sep.shape, jnp.float32),
-            jax.ShapeDtypeStruct((basis, vecs), jnp.float32),
-        ),
+        out_shape=tuple(jax.ShapeDtypeStruct(x.shape, x.dtype) for x in parts),
         in_specs=[anywhere] * 3,
-        out_specs=(anywhere, anywhere, vmem),
-        scratch_shapes=[wide(vecs, lanes), pltpu.SemaphoreType.DMA((3,))],
+        out_specs=(anywhere,) * 3,
+        scratch_shapes=[pltpu.VMEM(x.shape, x.dtype) for x in parts]
+        + [pltpu.SemaphoreType.DMA((3,))] * 2,
         compiler_params=pltpu.CompilerParams(vmem_limit_bytes=56 * 1024 * 1024),
     )(*parts)
+    return orth_sub, orth_sep, coef.T
 
 
 def apply_blocks(vectors, inverse):

time: 56.7 us -> 50.4 us (0.89)
  Pallas kernels: 53.8 us -> 49 us
  local copies, waits for them, and re-layouts: 1.4 us -> 0 us
    pallas_call x1, Pallas kernels: 5.7 us -> 1.55 us  [fused_shards(): pl.pallas_call(hand_over, out_shape=tuple((jax.ShapeDtypeStruct(x.shape,...]
    pallas_call x1 -> x0, local copies, waits for them, and re-layouts: 1.4 us -> none  [fused_shards(): pl.pallas_call(hand_over, out_shape=(jax.ShapeDtypeStruct(rhs_sub.shape,...]
    pallas_call x1, Pallas kernels: 48.1 us -> 47.4 us  [fused_shards(): pl.pallas_call(functools.partial(fused, leaves, fronts), out_shape=(jax.S...]
where the time goes in v3:
time: 50.4 us; the launch traced here: 50.2 us
  Pallas kernels  49 us (97%)
  between operations  1.29 us (3%)
    pallas_call x1, Pallas kernels, fused_shards(): pl.pallas_call(functools.partial(fused, leaves, fronts), out_shape=(jax.S...  47.4 us
    pallas_call x1, Pallas kernels, fused_shards(): pl.pallas_call(hand_over, out_shape=tuple((jax.ShapeDtypeStruct(x.shape,...  1.55 us

profile of v3, /device:TPU:0, one launch (start us, length us, event | category | flops | bytes accessed | tf_op | source)
XLA Modules:
  0.0 50.2 jit_solution(16375553805662557311)
XLA Ops:
  1.3 47.4 %shard_map.130 = (f32[8,2048]{1,0:T(8,128)}, f32[8,2048]{1,0:T(8,128)}, f32[8,48]{1,0:T(8,128)}) custom-call(s32[1]{0:T(128)S(6)} %copy.14.live_rows, f32[8,2048]{1,0:T(8,128)} %rhs_sub.1, f32[8,2048]{1,0:T(8,128)} %rhs_sep.1, bf16[8,256,256]{2,1,0:T(8,128)(2,1)} %lower_inv.1, bf16[8,256,256]{2,1,0:T(8,128)(2,1)} %upper_inv.1, bf16[64,16384]{1,0:T(8,128)(2,1)} %couple_low.1, ...), custom_call_target="tpu_custom_call" | custom-call | tf_op jit(solution)/shard_map/pallas_call | solution.py:412
  48.7 1.6 %shard_map.131 = (f32[8,2048]{1,0:T(8,128)}, f32[8,2048]{1,0:T(8,128)}, f32[8,48]{1,0:T(8,128)}) custom-call(f32[8,2048]{1,0:T(8,128)} %get-tuple-element.9.refs_0_, f32[8,2048]{1,0:T(8,128)} %get-tuple-element.10.refs_1_, f32[8,48]{1,0:T(8,128)} %get-tuple-element.11.refs_2_), custom_call_target="tpu_custom_call" | custom-call | tf_op jit(solution)/shard_map/pallas_call | solution.py:455

commit v4 on v3

--- a/solution.py
+++ b/solution.py
@@ -283,19 +283,24 @@
 
     def times_upper(piece, to):
         return lax.dot_general(
-            piece[0], sup_v[to, piece[1]], LAST, preferred_element_type=jnp.float32
+            sup_v[to, piece[1]], piece[0], LAST, preferred_element_type=jnp.float32
         )
 
     drain(sup_v, load.at[9])
-    for k in range(leaves - 2):
-        piece = low_piece(k)
+    for group in (range(0, 1), range(1, 2), range(2, leaves // 2)):
+        pieces = [low_piece(k) for k in group]
+        if not pieces:
+            continue
         for n in range(fronts):
-            product = times_upper(piece, slice(n * width, (n + 1) * width))
-            c_acc[n] = c_acc[n] + product if k else product
-    last2 = [low_piece(k) for k in range(leaves - 2, leaves)]
+            to = slice(n * width, (n + 1) * width)
+            product = sum(times_upper(piece, to) for piece in pieces)
+            c_acc[n] = c_acc[n] + product if group[0] else product
+    last2 = [low_piece(k) for k in range(max(2, leaves // 2), leaves)]
 
     def upper_piece(to):
-        return c_acc[to] + sum(times_upper(piece, strip(to)) for piece in last2)
+        return jnp.transpose(
+            c_acc[to] + sum(times_upper(piece, strip(to)) for piece in last2)
+        )
 
     for k in range(fronts - 1, 0, -1):
         to = flip(front, k)
@@ -350,15 +355,20 @@
     for k in range(leaves - 1, 0, -1):
         push(h_leaf.at[leaf], h_leaf.at[leaf], H_LEAF, (flip(leaf, k), front))
     drain(s_buf.at[pl.ds(0, fronts - 1)], recv.at[S_ALL])
+    rows_cols = (((1,), (0,)), ((), ()))
+    twice = 2.0 * (
+        lax.broadcasted_iota(jnp.int32, gram.shape, 0)
+        == lax.broadcasted_iota(jnp.int32, gram.shape, 1)
+    ).astype(jnp.float32) - gram
+    bsub_v[...] = exact(twice, bsub_v[...], rows_cols)
+    bsep_v[...] = exact(twice, bsep_v[...], rows_cols)
     drain(h_leaf.at[pl.ds(0, leaves - 1)], recv.at[H_LEAF])
 
     once = jnp.sum(h_leaf[...], axis=0)[:, 0:basis]
-    rows_cols = (((1,), (0,)), ((), ()))
-    both = once + (once - exact(once, gram, rows_cols))
-    coef[...] = both
-    orth_sub[...] = sol_v[...] - exact(both, bsub_v[...], rows_cols)
+    orth_sub[...] = sol_v[...] - exact(once, bsub_v[...], rows_cols)
     top_sol = jnp.concatenate([s_buf[k] for k in range(fronts)], axis=1)
-    orth_sep[...] = top_sol - exact(both, bsep_v[...], rows_cols)
+    orth_sep[...] = top_sol - exact(once, bsep_v[...], rows_cols)
+    coef[...] = once + (once - exact(once, gram, rows_cols))
 
     drain(a_pair, send.at[A_PAIR])
     drain(a_recv, send.at[A_SUM])
@@ -431,7 +441,7 @@
             wide(leaves - 1, vecs, width),
             wide(leaves - 1, vecs, width),
             slim(leaves),
-            wide(fronts, vecs, width),
+            wide(fronts, width, vecs),
             wide(fronts - 1, vecs, width),
             wide(fronts - 1, vecs, width),
             wide(fronts, vecs, width),

time: 50.4 us -> 49.8 us (0.988)
  Pallas kernels: 49 us -> 48.3 us
    pallas_call x1, Pallas kernels: 47.4 us -> 46.8 us  [fused_shards(): pl.pallas_call(functools.partial(fused, leaves, fronts), out_shape=(jax.S...]
where the time goes in v4:
time: 49.8 us; the launch traced here: 49.6 us
  Pallas kernels  48.3 us (97%)
  between operations  1.29 us (3%)
    pallas_call x1, Pallas kernels, fused_shards(): pl.pallas_call(functools.partial(fused, leaves, fronts), out_shape=(jax.S...  46.8 us
    pallas_call x1, Pallas kernels, fused_shards(): pl.pallas_call(hand_over, out_shape=tuple((jax.ShapeDtypeStruct(x.shape,...  1.55 us

profile of v4, /device:TPU:0, one launch (start us, length us, event | category | flops | bytes accessed | tf_op | source)
XLA Modules:
  0.0 49.6 jit_solution(17935313178331429677)
XLA Ops:
  1.3 46.8 %shard_map.130 = (f32[8,2048]{1,0:T(8,128)}, f32[8,2048]{1,0:T(8,128)}, f32[8,48]{1,0:T(8,128)}) custom-call(s32[1]{0:T(128)S(6)} %copy.14.live_rows, f32[8,2048]{1,0:T(8,128)} %rhs_sub.1, f32[8,2048]{1,0:T(8,128)} %rhs_sep.1, bf16[8,256,256]{2,1,0:T(8,128)(2,1)} %lower_inv.1, bf16[8,256,256]{2,1,0:T(8,128)(2,1)} %upper_inv.1, bf16[64,16384]{1,0:T(8,128)(2,1)} %couple_low.1, ...), custom_call_target="tpu_custom_call" | custom-call | tf_op jit(solution)/shard_map/pallas_call | solution.py:422
  48.0 1.6 %shard_map.131 = (f32[8,2048]{1,0:T(8,128)}, f32[8,2048]{1,0:T(8,128)}, f32[8,48]{1,0:T(8,128)}) custom-call(f32[8,2048]{1,0:T(8,128)} %get-tuple-element.9.refs_0_, f32[8,2048]{1,0:T(8,128)} %get-tuple-element.10.refs_1_, f32[8,48]{1,0:T(8,128)} %get-tuple-element.11.refs_2_), custom_call_target="tpu_custom_call" | custom-call | tf_op jit(solution)/shard_map/pallas_call | solution.py:465

commit v5 on v4

--- a/solution.py
+++ b/solution.py
@@ -255,11 +255,6 @@
         for n in range(leaves):
             product = times_lower(piece, slice(n * width, (n + 1) * width))
             b_acc[n] = b_acc[n] + product if k else product
-        if k == 0:
-            drain(g_front.at[pl.ds(0, fronts - 1)], recv.at[G_FRONT])
-            g_leaf[leaf] = jnp.sum(g_front[...], axis=0)
-            for j in range(1, leaves):
-                push(g_leaf.at[leaf], g_leaf.at[leaf], G_LEAF, (flip(leaf, j), front))
     last = [top_piece(k) for k in range(fronts - 2, fronts)]
 
     def lower_piece(to):
@@ -267,12 +262,12 @@
 
     for k in range(leaves - 1, 0, -1):
         to = flip(leaf, k)
-        b_send[k - 1] = lower_piece(to)
+        b_send[k - 1] = fold(lower_piece(to)).astype(jnp.bfloat16)
         push(b_send.at[k - 1], b_recv.at[k - 1], B_SUM, (to, front))
     piece = lower_piece(leaf)
     drain(b_recv, recv.at[B_SUM])
-    piece = piece + jnp.sum(b_recv[...], axis=0)
-    l_buf[0] = fold(piece).astype(jnp.bfloat16)
+    piece = fold(piece) + jnp.sum(b_recv[...].astype(jnp.float32), axis=0)
+    l_buf[0] = piece.astype(jnp.bfloat16)
     for k in range(leaves - 1, 0, -1):
         push(l_buf.at[0], l_buf.at[k], B_ALL, (flip(leaf, k), front), recv_leaf.at[k])
 
@@ -296,6 +291,10 @@
             product = sum(times_upper(piece, to) for piece in pieces)
             c_acc[n] = c_acc[n] + product if group[0] else product
     last2 = [low_piece(k) for k in range(max(2, leaves // 2), leaves)]
+    drain(g_front.at[pl.ds(0, fronts - 1)], recv.at[G_FRONT])
+    g_leaf[leaf] = jnp.sum(g_front[...], axis=0)
+    for k in range(1, leaves):
+        push(g_leaf.at[leaf], g_leaf.at[leaf], G_LEAF, (flip(leaf, k), front))
 
     def upper_piece(to):
         return jnp.transpose(
@@ -438,8 +437,8 @@
             slim(half - 1),
             slim(fronts),
             wide(leaves, vecs, width),
-            wide(leaves - 1, vecs, width),
-            wide(leaves - 1, vecs, width),
+            slim(leaves - 1),
+            slim(leaves - 1),
             slim(leaves),
             wide(fronts, width, vecs),
             wide(fronts - 1, vecs, width),

time: 49.8 us -> 47.2 us (0.948)
  Pallas kernels: 48.3 us -> 45.7 us
    pallas_call x1, Pallas kernels: 46.8 us -> 44.2 us  [fused_shards(): pl.pallas_call(functools.partial(fused, leaves, fronts), out_shape=(jax.S...]
where the time goes in v5:
time: 47.2 us; the launch traced here: 47 us
  Pallas kernels  45.7 us (97%)
  between operations  1.29 us (3%)
    pallas_call x1, Pallas kernels, fused_shards(): pl.pallas_call(functools.partial(fused, leaves, fronts), out_shape=(jax.S...  44.2 us
    pallas_call x1, Pallas kernels, fused_shards(): pl.pallas_call(hand_over, out_shape=tuple((jax.ShapeDtypeStruct(x.shape,...  1.55 us

profile of v5, /device:TPU:0, one launch (start us, length us, event | category | flops | bytes accessed | tf_op | source)
XLA Modules:
  0.0 47.0 jit_solution(17502952361186585664)
XLA Ops:
  1.3 44.2 %shard_map.130 = (f32[8,2048]{1,0:T(8,128)}, f32[8,2048]{1,0:T(8,128)}, f32[8,48]{1,0:T(8,128)}) custom-call(s32[1]{0:T(128)S(6)} %copy.14.live_rows, f32[8,2048]{1,0:T(8,128)} %rhs_sub.1, f32[8,2048]{1,0:T(8,128)} %rhs_sep.1, bf16[8,256,256]{2,1,0:T(8,128)(2,1)} %lower_inv.1, bf16[8,256,256]{2,1,0:T(8,128)(2,1)} %upper_inv.1, bf16[64,16384]{1,0:T(8,128)(2,1)} %couple_low.1, ...), custom_call_target="tpu_custom_call" | custom-call | tf_op jit(solution)/shard_map/pallas_call | solution.py:421
  45.4 1.6 %shard_map.131 = (f32[8,2048]{1,0:T(8,128)}, f32[8,2048]{1,0:T(8,128)}, f32[8,48]{1,0:T(8,128)}) custom-call(f32[8,2048]{1,0:T(8,128)} %get-tuple-element.9.refs_0_, f32[8,2048]{1,0:T(8,128)} %get-tuple-element.10.refs_1_, f32[8,48]{1,0:T(8,128)} %get-tuple-element.11.refs_2_), custom_call_target="tpu_custom_call" | custom-call | tf_op jit(solution)/shard_map/pallas_call | solution.py:464
